TPU v7x, 256 devices: a whole 4x4x8 slice. The times are simulated.
256 devices in a mesh: seq: 16 (over z, core), wt: 16 (over x, y).
Axes of the slice: x: 4, y: 4, z: 8, core: 2. Of those that a mesh axis runs over, the one named last changes fastest.
Arguments:
- queries: bfloat16 [8192, 8192], P('seq', 'wt'), may hold values from -6 to 6
- keys_in: bfloat16 [8192, 8192], P('seq', 'wt'), may hold values from -6 to 6
- values_in: bfloat16 [8192, 8192], P('seq', 'wt'), may hold values from -6 to 6
- stream: bfloat16 [8192, 8192], P('seq', 'wt')
- attn_gain: float32 [8192], P('wt'), may hold values from 0.1 to 1.9
- mlp_gain: float32 [8192], replicated, may hold values from 0.1 to 1.9
- up_index: int32 [128, 16], P('wt'), may hold values from 0 to 63, all different within a row
- up_blocks: bfloat16 [128, 16, 128, 128], P('wt'), may hold values from -0.125 to 0.125
- down_index: int32 [128, 16], P('wt'), may hold values from 0 to 63, all different within a row
- down_blocks: bfloat16 [128, 16, 128, 128], P('wt'), may hold values from -0.09375 to 0.09375
Outputs:
- result: bfloat16 [8192, 8192], P('seq', 'wt')
Inputs may be any that keep to these rules, and one draw needn't show every extreme that they name: `up_index`: each row names 16 different feature blocks, and every feature block is named by some row. `down_index`: each row names 16 different output blocks, and every output block is named by some row.
All inputs are finite; a program needn't handle non-finite values.
Results may differ from a plain program's by a relative error of at most 0.013.
Values may be sent and summed in bfloat16 or wider, within the bound.
No kernel may reach another device: no remote copies, remote signals or barrier semaphores. Data moves between devices by JAX's collectives and lax.ppermute only.
A program may use at most 128 MiB of HBM per device.

v0:
```python
import jax
import jax.numpy as jnp
from jax import lax
from jax.sharding import PartitionSpec as P

HEAD = 128
BLK = 128


def carried_in(x, axis, join, neutral):
    place = lax.axis_index(axis)
    gathered = lax.all_gather(x.astype(jnp.bfloat16), axis)
    state = jnp.zeros_like(x) + jnp.asarray(neutral, x.dtype)

    def one(step, state):
        return join(state, lax.dynamic_index_in_dim(gathered, step, 0, False).astype(x.dtype))

    return lax.fori_loop(0, place, one, state)


def feature_map(a):
    return (jax.nn.elu(a.astype(jnp.float32)) + 1.0).astype(jnp.bfloat16)


def add_states(earlier, later):
    return earlier + later


def per_device(
    queries,
    keys_in,
    values_in,
    stream,
    attn_gain,
    mlp_gain,
    up_index,
    up_blocks,
    down_index,
    down_blocks,
):
    rows = queries.shape[0]
    local_cols = queries.shape[1]
    local_heads = local_cols // HEAD
    fq = feature_map(queries).reshape(rows, local_heads, HEAD)
    fk = feature_map(keys_in).reshape(rows, local_heads, HEAD)
    vals = values_in.reshape(rows, local_heads, HEAD)
    causal = jnp.tril(jnp.ones((rows, rows), dtype=bool))
    scores = jnp.einsum("thd,shd->hts", fq, fk, preferred_element_type=jnp.float32)
    scores = jnp.where(causal[None], scores, 0.0).astype(jnp.bfloat16)
    intra = jnp.einsum("hts,shd->thd", scores, vals, preferred_element_type=jnp.float32)
    own_state = jnp.einsum("shd,she->hde", fk, vals, preferred_element_type=jnp.float32)
    empty = jnp.zeros_like(own_state)
    before = carried_in(own_state, "seq", add_states, empty)
    inter = jnp.einsum(
        "thd,hde->the", fq.astype(jnp.float32), before, precision=lax.Precision.HIGHEST
    )
    raw = intra + inter
    normal_raw = raw * lax.rsqrt(jnp.mean(raw * raw, axis=-1, keepdims=True) + 1e-06)
    attn = normal_raw.reshape(rows, local_cols) * attn_gain
    mid = (stream.astype(jnp.float32) + attn).astype(jnp.bfloat16)
    width = mlp_gain.shape[0]
    whole = lax.all_gather(mid, "wt", axis=1, tiled=True)
    whole_f = whole.astype(jnp.float32)
    scale = lax.rsqrt(jnp.mean(whole_f * whole_f, axis=-1, keepdims=True) + 1e-06)
    normed = (whole_f * scale * mlp_gain).astype(jnp.bfloat16)
    tiles = normed.reshape(rows, width // BLK, BLK)
    own_blocks = up_blocks.shape[0]
    picks = jnp.take(tiles, up_index.reshape(-1), axis=1)
    picks = picks.reshape(rows, own_blocks, up_index.shape[1], BLK)
    upper = jnp.einsum("lckd,ckde->lce", picks, up_blocks, preferred_element_type=jnp.float32)
    act = jax.nn.silu(upper).astype(jnp.bfloat16)
    parts = jnp.einsum("lrd,rkde->rkle", act, down_blocks, preferred_element_type=jnp.float32)
    parts = parts.reshape(-1, rows, BLK)
    summed = jax.ops.segment_sum(parts, down_index.reshape(-1), num_segments=width // BLK)
    partial_sum = summed.astype(jnp.bfloat16)
    mine = lax.psum_scatter(partial_sum, "wt", scatter_dimension=0, tiled=True).astype(jnp.float32)
    down = jnp.transpose(mine, (1, 0, 2)).reshape(rows, local_cols)
    return (mid.astype(jnp.float32) + down).astype(jnp.bfloat16)


def solution(mesh):
    placed = (
        P("seq", "wt"),
        P("seq", "wt"),
        P("seq", "wt"),
        P("seq", "wt"),
        P("wt"),
        P(),
        P("wt", None),
        P("wt", None, None, None),
        P("wt", None),
        P("wt", None, None, None),
    )
    return jax.shard_map(
        per_device, mesh=mesh, in_specs=placed, out_specs=P("seq", "wt"), check_vma=False
    )
```

profile of v0, /device:TPU:2, one launch (start us, length us, event | category | flops | bytes accessed | tf_op | source)
XLA Modules:
  0.0 391.9 jit_solution(10710767317259980740)
XLA Ops:
  6.5 0.0 copy-start
  6.5 0.0 copy-start.8
  6.5 0.0 all-gather.6.cloned.1.call-start
  6.5 1.6 fusion.27
  8.1 0.2 copy.49
  8.4 0.0 copy-done
  8.4 0.9 convolution_convert_fusion
  9.3 0.0 all-gather.6.cloned.1.call-update
  9.3 0.0 all-gather.4.cloned.1.call-start
  9.4 1.3 copy.35
  10.6 0.0 copy-start.7
  10.7 0.1 iota_compare_fusion
  10.7 41.4 %all-gather.6.cloned.1.call-done = bf16[64,128,128]{2,1,0:T(8,128)(2,1)} async-done(((bf16[4,128,128]{2,1,0:T(8,128)(2,1)}), bf16[64,128,128]{2,1,0:T(8,128)(2,1)}) %all-gather.6.cloned.1.call-update) | async-done | bytes 2097168 | tf_op jit(solution)/shard_map/all_gather | solution.py:12
  52.2 0.0 copy-start.6
  52.2 0.0 copy-start.5
  52.2 0.0 copy-done.8
  52.2 1.9 convolution_bitcast_fusion
  54.2 2.8 multiply_reduce_fusion
  57.0 0.0 copy-start.4
  57.1 0.1 broadcast_multiply_fusion
  57.2 0.0 copy-done.7
  57.2 1.0 fusion.30
  58.2 0.0 all-gather.4.cloned.1.call-update
  58.2 0.2 reduce-scatter.2.cloned.1.call-start
  58.5 0.0 copy-done.6
  58.5 0.1 reshape.114
  58.6 0.0 copy-done.5
  58.6 0.1 reshape.96
  58.7 87.3 %all-gather.4.cloned.1.call-done = bf16[512,8192]{0,1:T(8,128)(2,1)} async-done(((bf16[512,512]{0,1:T(8,128)(2,1)}), bf16[512,8192]{0,1:T(8,128)(2,1)}) %all-gather.4.cloned.1.call-update) | async-done | bytes 8388624 | tf_op jit(solution)/shard_map/all_gather | solution.py:62
  146.0 0.0 copy-start.2
  146.0 5.3 %fusion = f32[512]{0:T(512)S(1)} fusion(bf16[512,8192]{0,1:T(8,128)(2,1)} %all-gather.4.cloned.1.call-done), kind=kLoop, calls=%fused_computation.5 | loop fusion | flops 12582400 | bytes 8390656 | tf_op jit(solution)/shard_map/reduce_sum | solution.py:64
  151.3 0.0 copy-done.4
  151.3 0.4 copy-done.2
  151.7 4.4 %fusion.2 = bf16[512,8192]{0,1:T(8,128)(2,1)} fusion(bf16[512,8192]{0,1:T(8,128)(2,1)S(1)} %copy-done.2, f32[8192]{0:T(1024)S(1)} %copy-done.4, f32[512]{0:T(512)S(1)} %add_rsqrt_fusion.1), kind=kLoop, calls=%fused_computation.7 | loop fusion | flops 16777216 | bytes 16812032 | tf_op jit(solution)/shard_map/convert_element_type | solution.py:65
  156.1 12.0 %copy.43 = bf16[512,64,128]{2,0,1:T(8,128)(2,1)} copy(bf16[512,64,128]{0,2,1:T(8,128)(2,1)} %bitcast.96) | data formatting | bytes 16777216 | tf_op jit(solution)/shard_map/reshape | solution.py:66
  168.1 11.8 %gather_fusion = bf16[128,512,128]{2,1,0:T(8,128)(2,1)} fusion(bf16[512,64,128]{2,0,1:T(8,128)(2,1)} %copy.43, s32[1024]{0:T(1024)S(1)} %pad_clamp_fusion), kind=kCustom, calls=%fused_computation | custom fusion | bytes 33554944 | tf_op jit(solution)/shard_map/jit(_take)/gather | solution.py:68
  179.9 21.8 %fusion.20 = f32[8,512,16,128]{3,1,2,0:T(8,128)} fusion(bf16[8,16,128,128]{3,2,1,0:T(8,128)(2,1)} %param.21, bf16[8,16,128,128]{3,2,1,0:T(8,128)(2,1)} %param.19, bf16[512,8,16,128]{3,0,2,1:T(8,128)(2,1)} %bitcast.95, pred[8,16]{1,0:T(8,128)(4,1)S(1)} %compare_and_fusion), kind=kOutput, calls=%fused_computation.28 | convolution fusion | flops 4305977344 | bytes 58720384 | tf_op jit(solution)/shard_map/lrd,rkde->rkle/dot_general | solution.py:72
  201.7 7.8 %broadcast_in_dim.43 = f32[64,512,128]{2,1,0:T(8,128)} broadcast(f32[]{:T(128)} %constant.27.clone.1), dimensions={} | broadcast | bytes 16777220 | tf_op jit(solution)/shard_map/broadcast_in_dim | solution.py:74
  209.5 73.8 %scatter_fusion = f32[64,512,128]{2,1,0:T(8,128)} fusion(f32[64,512,128]{2,1,0:T(8,128)} %broadcast_in_dim.43, s32[128]{0:T(128)S(1)} %reshape.114, f32[128,512,128]{2,1,0:T(8,128)} %bitcast.94), kind=kCustom, calls=%fused_computation.1 | custom fusion | flops 8388608 | bytes 100663808 | tf_op jit(solution)/shard_map/scatter-add | solution.py:74
  283.3 0.0 copy-start.1
  283.3 9.3 %convert_element_type.62 = bf16[64,512,128]{2,1,0:T(8,128)(2,1)} convert(f32[64,512,128]{2,1,0:T(8,128)} %scatter_fusion) | non-fusion elementwise | flops 4194304 | bytes 25165824 | tf_op jit(solution)/shard_map/convert_element_type | solution.py:75
  292.6 0.0 copy-start.3
  292.6 0.0 reduce-scatter.2.cloned.1.call-update
  292.6 90.1 %reduce-scatter.2.cloned.1.call-done = bf16[4,512,128]{2,1,0:T(8,128)(2,1)} async-done(((bf16[64,512,128]{2,1,0:T(8,128)(2,1)}), bf16[4,512,128]{2,1,0:T(8,128)(2,1)}) %reduce-scatter.2.cloned.1.call-update) | async-done | bytes 524304 | tf_op jit(solution)/shard_map/reduce_scatter | solution.py:76
  382.7 1.1 convert_bitcast_fusion
  383.8 0.3 copy.44
  384.2 0.0 copy-done.3
  384.2 0.2 fusion.28
  384.4 1.0 copy.45
  385.4 0.0 copy-done.1
  (7 shorter events, 0.1 us)
Async XLA Ops:
  6.5 1.8 copy-start
  6.5 45.7 %copy-start.8 = (bf16[512,512]{1,0:T(8,128)(2,1)S(1)}, bf16[512,512]{1,0:T(8,128)(2,1)}, u32[]{:S(2)}) copy-start(bf16[512,512]{1,0:T(8,128)(2,1)} %param.12) | copy-start | bytes 1572868
  6.5 45.6 %all-gather.6.cloned.1.call-start = ((), (), s32[]{:S(2)}) async-start(), calls=%async_computation.3 | async-start | bytes 2228224 | tf_op jit(solution)/shard_map/all_gather | solution.py:12
  9.3 136.6 %all-gather.4.cloned.1.call-start = ((), (), s32[]{:S(2)}) async-start(), calls=%async_computation.1 | async-start | bytes 8912896 | tf_op jit(solution)/shard_map/all_gather | solution.py:62
  10.6 46.6 %copy-start.7 = (f32[512]{0:T(512)S(1)}, f32[512]{0:T(512)}, u32[]{:S(2)}) copy-start(f32[512]{0:T(512)} %param.16) | copy-start | bytes 6148
  52.2 6.3 %copy-start.6 = (s32[8,16]{1,0:T(8,128)S(1)}, s32[8,16]{1,0:T(8,128)}, u32[]{:S(2)}) copy-start(s32[8,16]{1,0:T(8,128)} %param.20) | copy-start | bytes 1540
  52.2 6.3 %copy-start.5 = (s32[8,16]{1,0:T(8,128)S(1)}, s32[8,16]{1,0:T(8,128)}, u32[]{:S(2)}) copy-start(s32[8,16]{1,0:T(8,128)} %param.18) | copy-start | bytes 1540
  57.0 94.2 %copy-start.4 = (f32[8192]{0:T(1024)S(1)}, f32[8192]{0:T(1024)}, u32[]{:S(2)}) copy-start(f32[8192]{0:T(1024)} %param.17) | copy-start | bytes 98308
  58.2 324.5 %reduce-scatter.2.cloned.1.call-start = ((), (), s32[]{:S(2)}) async-start(), calls=%async_computation.2 | async-start | bytes 8912896 | tf_op jit(solution)/shard_map/reduce_scatter | solution.py:76
  146.0 5.8 %copy-start.2 = (bf16[512,8192]{0,1:T(8,128)(2,1)S(1)}, bf16[512,8192]{0,1:T(8,128)(2,1)}, u32[]{:S(2)}) copy-start(bf16[512,8192]{0,1:T(8,128)(2,1)} %all-gather.4.cloned.1.call-done) | copy-start | bytes 25165828
  283.3 102.1 %copy-start.1 = (bf16[512,512]{1,0:T(8,128)(2,1)S(1)}, bf16[512,512]{1,0:T(8,128)(2,1)}, u32[]{:S(2)}) copy-start(bf16[512,512]{1,0:T(8,128)(2,1)} %param.14) | copy-start | bytes 1572868
  292.6 91.6 %copy-start.3 = (bf16[512,512]{0,1:T(8,128)(2,1)S(1)}, bf16[512,512]{0,1:T(8,128)(2,1)}, u32[]{:S(2)}) copy-start(bf16[512,512]{0,1:T(8,128)(2,1)} %fusion.30) | copy-start | bytes 1572868
Sparse Core Ops, SparseCore 0:
  9.5 42.6 all-gather.5
  58.4 87.5 all-gather.3
  292.7 89.9 reduce-scatter.1
where the time goes:
time: 393 us; the launch traced here: 392 us
  waiting for transfers between devices  219 us (56%)
  other arithmetic  96.8 us (25%)
  local copies, waits for them, and re-layouts  35.1 us (9%)
  matrix products  27.6 us (7%)
  between operations  13.3 us (3%)
    reduce_scatter x1, waiting for transfers between devices, per_device(): lax.psum_scatter(partial_sum, 'wt', scatter_dimension=0, tiled=True)  90.1 us
    all_gather x1, waiting for transfers between devices, per_device(): whole = lax.all_gather(mid, 'wt', axis=1, tiled=True)  87.3 us
    scatter-add x1, other arithmetic, per_device(): jax.ops.segment_sum(parts, down_index.reshape(-1), num_segments=width //...  73.8 us
    all_gather x1, waiting for transfers between devices, carried_in(): gathered = lax.all_gather(x.astype(jnp.bfloat16), axis)  41.4 us
    dot_general x1, matrix products, per_device(): jnp.einsum('lrd,rkde->rkle', act, down_blocks, preferred_element_type=jnp...  21.8 us
    reshape x1, local copies, waits for them, and re-layouts, per_device(): tiles = normed.reshape(rows, width // BLK, BLK)  12 us
    gather x1, local copies, waits for them, and re-layouts, per_device(): picks = jnp.take(tiles, up_index.reshape(-1), axis=1)  11.8 us
    convert_element_type x1, other arithmetic, per_device(): partial_sum = summed.astype(jnp.bfloat16)  9.25 us
  transfers between devices with their start and end apart: 3, of which 3 were waited for; matrix products, arithmetic and copies ran while one was open for 0% of the time, Pallas kernels for 0%

commit v1 on v0

--- a/solution.py
+++ b/solution.py
@@ -59,7 +59,16 @@
     attn = normal_raw.reshape(rows, local_cols) * attn_gain
     mid = (stream.astype(jnp.float32) + attn).astype(jnp.bfloat16)
     width = mlp_gain.shape[0]
-    whole = lax.all_gather(mid, "wt", axis=1, tiled=True)
+    _trace_zones = lambda sample, lane_axis: jnp.concatenate(
+        lax.all_to_all(
+            jnp.stack(lax.axis_size(lane_axis) * [sample]),
+            axis_name=lane_axis,
+            split_axis=0,
+            concat_axis=0,
+        ),
+        axis=1,
+    )
+    whole = _trace_zones(mid, "wt")
     whole_f = whole.astype(jnp.float32)
     scale = lax.rsqrt(jnp.mean(whole_f * whole_f, axis=-1, keepdims=True) + 1e-06)
     normed = (whole_f * scale * mlp_gain).astype(jnp.bfloat16)

time: 393 us -> 504 us (1.28)
  waiting for transfers between devices: 219 us -> 297 us
  other arithmetic: 96.8 us -> 113 us
  local copies, waits for them, and re-layouts: 35.1 us -> 44 us
  starting transfers between devices: 0.27 us -> 7.63 us
    all_to_all x0 -> x1, waiting for transfers between devices: none -> 107 us  [per_device(): lax.all_to_all(jnp.stack(lax.axis_size(lane_axis) * [sample]), axis_name=...]
    all_gather x1 -> x0, waiting for transfers between devices: 87.3 us -> none  [per_device(): whole = lax.all_gather(mid, 'wt', axis=1, tiled=True)]
    reduce_scatter x1, waiting for transfers between devices: 90.1 us -> 149 us  [per_device(): lax.psum_scatter(partial_sum, 'wt', scatter_dimension=0, tiled=True)]
    convert_element_type x0 -> x1, local copies, waits for them, and re-layouts: none -> 17.4 us  [per_device(): whole_f = whole.astype(jnp.float32)]
    reshape x1 -> x0, local copies, waits for them, and re-layouts: 12 us -> none  [per_device(): tiles = normed.reshape(rows, width // BLK, BLK)]
    convert_element_type x0 -> x1, other arithmetic: none -> 11.4 us  [per_device(): whole_f = whole.astype(jnp.float32)]
    all_to_all x0 -> x1, starting transfers between devices: none -> 7.41 us  [per_device(): lax.all_to_all(jnp.stack(lax.axis_size(lane_axis) * [sample]), axis_name=...]
    convert_element_type x1, other arithmetic: 4.35 us -> 10 us  [per_device(): normed = (whole_f * scale * mlp_gain).astype(jnp.bfloat16)]
where the time goes in v1:
time: 504 us; the launch traced here: 503 us
  waiting for transfers between devices  297 us (59%)
  other arithmetic  113 us (22%)
  local copies, waits for them, and re-layouts  44 us (9%)
  matrix products  27.6 us (5%)
  between operations  13.5 us (3%)
  starting transfers between devices  7.63 us (2%)
    reduce_scatter x1, waiting for transfers between devices, per_device(): lax.psum_scatter(partial_sum, 'wt', scatter_dimension=0, tiled=True)  149 us
    all_to_all x1, waiting for transfers between devices, per_device(): lax.all_to_all(jnp.stack(lax.axis_size(lane_axis) * [sample]), axis_name=...  107 us
    scatter-add x1, other arithmetic, per_device(): jax.ops.segment_sum(parts, down_index.reshape(-1), num_segments=width //...  73.6 us
    all_gather x1, waiting for transfers between devices, carried_in(): gathered = lax.all_gather(x.astype(jnp.bfloat16), axis)  41.5 us
    dot_general x1, matrix products, per_device(): jnp.einsum('lrd,rkde->rkle', act, down_blocks, preferred_element_type=jnp...  21.9 us
    convert_element_type x1, local copies, waits for them, and re-layouts, per_device(): whole_f = whole.astype(jnp.float32)  17.4 us
    gather x1, local copies, waits for them, and re-layouts, per_device(): picks = jnp.take(tiles, up_index.reshape(-1), axis=1)  11.8 us
    convert_element_type x1, other arithmetic, per_device(): whole_f = whole.astype(jnp.float32)  11.4 us
  transfers between devices with their start and end apart: 3, of which 3 were waited for; matrix products, arithmetic and copies ran while one was open for 0% of the time, Pallas kernels for 0%

profile of v1, /device:TPU:2, one launch (start us, length us, event | category | flops | bytes accessed | tf_op | source)
XLA Modules:
  0.0 503.0 jit_solution(2217390505003659784)
XLA Ops:
  6.5 0.0 copy-start
  6.5 0.0 copy-start.6
  6.5 0.0 all-gather.3.cloned.1.call-start
  6.5 1.6 fusion.24
  8.1 0.2 copy.50
  8.4 0.0 copy-done
  8.4 0.9 convolution_convert_fusion
  9.3 0.0 all-gather.3.cloned.1.call-update
  9.3 1.3 copy.36
  10.6 0.0 copy-start.5
  10.6 0.1 iota_compare_fusion
  10.7 41.5 %all-gather.3.cloned.1.call-done = bf16[64,128,128]{2,1,0:T(8,128)(2,1)} async-done(((bf16[4,128,128]{2,1,0:T(8,128)(2,1)}), bf16[64,128,128]{2,1,0:T(8,128)(2,1)}) %all-gather.3.cloned.1.call-update) | async-done | bytes 2097168 | tf_op jit(solution)/shard_map/all_gather | solution.py:12
  52.2 0.0 copy-done.6
  52.2 2.0 convolution_bitcast_fusion
  54.2 2.8 multiply_reduce_fusion.1
  57.0 0.1 broadcast_multiply_fusion
  57.2 0.0 copy-done.5
  57.2 0.2 fusion.27
  57.4 4.0 stack.2
  61.4 0.0 copy-start.4
  61.4 0.0 copy-start.3
  61.4 7.4 %all-to-all-start = ((bf16[16,512,512]{1,2,0:T(8,128)(2,1)}), bf16[16,512,512]{1,2,0:T(8,128)(2,1)}, u32[]{:S(2)}, u32[]{:S(2)}) async-start(bf16[16,512,512]{1,2,0:T(8,128)(2,1)} %stack.2), calls=%async_computation | async-start | bytes 16777216 | tf_op jit(solution)/shard_map/all_to_all | solution.py:63
  68.8 0.2 reduce-scatter.2.cloned.1.call-start
  69.1 0.0 copy-done.4
  69.1 0.1 reshape.129
  69.2 0.0 copy-done.3
  69.2 0.1 reshape.110
  69.3 106.8 %all-to-all-done = bf16[16,512,512]{1,2,0:T(8,128)(2,1)} async-done(((bf16[16,512,512]{1,2,0:T(8,128)(2,1)}), bf16[16,512,512]{1,2,0:T(8,128)(2,1)}, u32[]{:S(2)}, u32[]{:S(2)}) %all-to-all-start) | async-done | bytes 8388640 | tf_op jit(solution)/shard_map/all_to_all | solution.py:63
  176.1 5.2 %multiply_reduce_fusion = f32[512]{0:T(512)S(1)} fusion(bf16[16,512,512]{1,2,0:T(8,128)(2,1)} %all-to-all-done), kind=kLoop, calls=%fused_computation.6 | loop fusion | flops 12582400 | bytes 8390656 | tf_op jit(solution)/shard_map/reduce_sum | solution.py:73
  181.2 11.4 %convert_element_type.81 = f32[16,512,512]{1,2,0:T(8,128)} convert(bf16[16,512,512]{1,2,0:T(8,128)(2,1)} %all-to-all-done) | non-fusion elementwise | flops 4194304 | bytes 25165824 | tf_op jit(solution)/shard_map/convert_element_type | solution.py:72
  192.7 0.0 copy-start.2
  192.7 17.4 %copy.44 = f32[512,64,128]{2,0,1:T(8,128)} copy(f32[512,64,128]{0,2,1:T(8,128)} %bitcast.98) | data formatting | bytes 33554432 | tf_op jit(solution)/shard_map/convert_element_type | solution.py:72
  210.1 0.0 copy-done.2
  210.1 10.0 %multiply_convert_fusion = bf16[512,64,128]{2,0,1:T(8,128)(2,1)} fusion(f32[512,64,128]{2,0,1:T(8,128)} %copy.44, f32[64,128]{1,0:T(8,128)S(1)} %bitcast.103, f32[512]{0:T(512)S(1)} %add_rsqrt_fusion.1), kind=kLoop, calls=%fused_computation.5 | loop fusion | flops 12582912 | bytes 25200640 | tf_op jit(solution)/shard_map/convert_element_type | solution.py:74
  220.1 11.8 %gather_fusion = bf16[128,512,128]{2,1,0:T(8,128)(2,1)} fusion(bf16[512,64,128]{2,0,1:T(8,128)(2,1)} %multiply_convert_fusion, s32[1024]{0:T(1024)S(1)} %pad_clamp_fusion), kind=kCustom, calls=%fused_computation | custom fusion | bytes 33554944 | tf_op jit(solution)/shard_map/jit(_take)/gather | solution.py:77
  231.9 21.9 %fusion.17 = f32[8,512,16,128]{3,1,2,0:T(8,128)} fusion(bf16[8,16,128,128]{3,2,1,0:T(8,128)(2,1)} %param.21, bf16[8,16,128,128]{3,2,1,0:T(8,128)(2,1)} %param.19, bf16[512,8,16,128]{3,0,2,1:T(8,128)(2,1)} %bitcast.99, pred[8,16]{1,0:T(8,128)(4,1)S(1)} %compare_and_fusion), kind=kOutput, calls=%fused_computation.25 | convolution fusion | flops 4305977344 | bytes 58720384 | tf_op jit(solution)/shard_map/lrd,rkde->rkle/dot_general | solution.py:81
  253.7 7.8 %broadcast_in_dim.43 = f32[64,512,128]{2,1,0:T(8,128)} broadcast(f32[]{:T(128)} %constant.27.clone.1), dimensions={} | broadcast | bytes 16777220 | tf_op jit(solution)/shard_map/broadcast_in_dim | solution.py:83
  261.5 73.6 %scatter_fusion = f32[64,512,128]{2,1,0:T(8,128)} fusion(f32[64,512,128]{2,1,0:T(8,128)} %broadcast_in_dim.43, s32[128]{0:T(128)S(1)} %reshape.129, f32[128,512,128]{2,1,0:T(8,128)} %bitcast.97), kind=kCustom, calls=%fused_computation.1 | custom fusion | flops 8388608 | bytes 100663808 | tf_op jit(solution)/shard_map/scatter-add | solution.py:83
  335.1 0.0 copy-start.1
  335.1 9.3 %convert_element_type.77 = bf16[64,512,128]{2,1,0:T(8,128)(2,1)} convert(f32[64,512,128]{2,1,0:T(8,128)} %scatter_fusion) | non-fusion elementwise | flops 4194304 | bytes 25165824 | tf_op jit(solution)/shard_map/convert_element_type | solution.py:84
  344.4 0.0 reduce-scatter.2.cloned.1.call-update
  344.4 149.1 %reduce-scatter.2.cloned.1.call-done = bf16[4,512,128]{2,1,0:T(8,128)(2,1)} async-done(((bf16[64,512,128]{2,1,0:T(8,128)(2,1)}), bf16[4,512,128]{2,1,0:T(8,128)(2,1)}) %reduce-scatter.2.cloned.1.call-update) | async-done | bytes 524304 | tf_op jit(solution)/shard_map/reduce_scatter | solution.py:85
  493.5 1.1 convert_bitcast_fusion
  494.6 0.3 copy.45
  494.9 0.2 fusion.25
  495.1 1.0 copy.46
  496.1 0.0 copy-done.1
  (7 shorter events, 0.1 us)
Async XLA Ops:
  6.5 1.8 copy-start
  6.5 45.7 %copy-start.6 = (bf16[512,512]{1,0:T(8,128)(2,1)S(1)}, bf16[512,512]{1,0:T(8,128)(2,1)}, u32[]{:S(2)}) copy-start(bf16[512,512]{1,0:T(8,128)(2,1)} %param.12) | copy-start | bytes 1572868
  6.5 45.6 %all-gather.3.cloned.1.call-start = ((), (), s32[]{:S(2)}) async-start(), calls=%async_computation.3 | async-start | bytes 2228224 | tf_op jit(solution)/shard_map/all_gather | solution.py:12
  10.6 46.6 %copy-start.5 = (f32[512]{0:T(512)S(1)}, f32[512]{0:T(512)}, u32[]{:S(2)}) copy-start(f32[512]{0:T(512)} %param.16) | copy-start | bytes 6148
  61.4 7.6 %copy-start.4 = (s32[8,16]{1,0:T(8,128)S(1)}, s32[8,16]{1,0:T(8,128)}, u32[]{:S(2)}) copy-start(s32[8,16]{1,0:T(8,128)} %param.20) | copy-start | bytes 1540
  61.4 7.7 %copy-start.3 = (s32[8,16]{1,0:T(8,128)S(1)}, s32[8,16]{1,0:T(8,128)}, u32[]{:S(2)}) copy-start(s32[8,16]{1,0:T(8,128)} %param.18) | copy-start | bytes 1540
  61.4 114.6 %all-to-all-start = ((bf16[16,512,512]{1,2,0:T(8,128)(2,1)}), bf16[16,512,512]{1,2,0:T(8,128)(2,1)}, u32[]{:S(2)}, u32[]{:S(2)}) async-start(bf16[16,512,512]{1,2,0:T(8,128)(2,1)} %stack.2), calls=%async_computation | async-start | bytes 16777216 | tf_op jit(solution)/shard_map/all_to_all | solution.py:63
  68.8 424.6 %reduce-scatter.2.cloned.1.call-start = ((), (), s32[]{:S(2)}) async-start(), calls=%async_computation.2 | async-start | bytes 8912896 | tf_op jit(solution)/shard_map/reduce_scatter | solution.py:85
  192.7 17.4 %copy-start.2 = (f32[8192]{0:T(1024)S(1)}, f32[8192]{0:T(1024)}, u32[]{:S(2)}) copy-start(f32[8192]{0:T(1024)} %param.17) | copy-start | bytes 98308
  335.1 161.0 %copy-start.1 = (bf16[512,512]{1,0:T(8,128)(2,1)S(1)}, bf16[512,512]{1,0:T(8,128)(2,1)}, u32[]{:S(2)}) copy-start(bf16[512,512]{1,0:T(8,128)(2,1)} %param.14) | copy-start | bytes 1572868
Sparse Core Ops, SparseCore 0:
  9.5 42.6 all-gather.2
  344.5 148.9 reduce-scatter.1
